TPU v7x, 512 devices: a whole 4x8x8 slice. The times are simulated.
512 devices in a mesh: grp: 16 (over x, z_lo), mem: 32 (over z_hi, y, core).
Axes of the slice: x: 4, y: 8, z: 8 (z_hi: 2, z_lo: 4; z = z_hi * 4 + z_lo), core: 2. Of those that a mesh axis runs over, the one named last changes fastest.
Arguments:
- points: float32 [16, 262144], P(None, ('grp', 'mem')), may hold values from -6 to 6
- lengthscales: float32 [16], replicated, may hold values from 3 to 12
- probes: float32 [8, 262144], P(None, ('grp', 'mem')), may hold values from -0.25 to 0.25
- plan: int32 [16, 16], replicated, may hold values from 0 to 15, as said below
- round_index: int32 [1], replicated, may hold values from 0 to 15
Outputs:
- product: float32 [8, 262144], P(None, ('grp', 'mem'))
Inputs may be any that keep to these rules, and one draw needn't show every extreme that they name: plan[r, g] = g XOR t_r for one t_r of 1 to 15 in each round r, the same for all g, so that each round's pairing is a perfect matching without fixed points.
All inputs are finite; a program needn't handle non-finite values.
Results may differ from a plain program's by a relative error of at most 0.0003.
Values sent between devices are 32-bit elements; how exact they have to be, the bound alone decides.
A program may use at most 64 MiB of HBM per device.

v0:
```python
import functools
import math

import jax
import jax.numpy as jnp
from jax import lax
from jax.experimental import pallas as pl
from jax.experimental.pallas import tpu as pltpu
from jax.sharding import PartitionSpec as P

F32, BF16 = jnp.float32, jnp.bfloat16
MESH = pl.DeviceIdType.MESH
LOG2E = math.log2(math.e)
UNIT = math.sqrt(LOG2E / 3.0)
SCALE = math.sqrt(5.0) * UNIT
SLOPE = -LOG2E / UNIT
SHIFT = 3.0 * UNIT * UNIT

FEAT, PROBES, PTS = 16, 8, 512
ROWS = FEAT + PROBES
DEPTH = 128
RING, CORES, HALVES = 8, 2, 2


def coordinates():
    grp, mem = lax.axis_index("grp"), lax.axis_index("mem")
    return grp, mem // (RING * CORES), (mem // CORES) % RING, mem % CORES


def member(grp, half, ring, core):
    return (grp, (half * RING + ring) * CORES + core)


def near_devices():
    grp, half, ring, core = coordinates()
    return [
        member(grp, half, ring, 1 - core),
        member(grp, 1 - half, ring, core),
        member(grp, 1 - half, ring, 1 - core),
    ]


def remote(src, dst, send_sem, recv_sem, device):
    return pltpu.make_async_remote_copy(
        src_ref=src, dst_ref=dst, send_sem=send_sem, recv_sem=recv_sem,
        device_id=device, device_id_type=MESH,
    )


def enter(devices):
    barrier = pltpu.get_barrier_semaphore()
    for device in devices:
        pl.semaphore_signal(barrier, inc=1, device_id=device, device_id_type=MESH)
    return barrier


def scale_kernel(round_ref, plan_ref, ls_ref, pts_ref, prb_ref, shift_ref, own_ref):
    shift_ref[0] = plan_ref[round_ref[0], 0] - 1
    row = lax.broadcasted_iota(jnp.int32, (FEAT, PTS), 0)
    scales = jnp.full((FEAT, PTS), ls_ref[0], F32)
    for feature in range(1, FEAT):
        scales = jnp.where(row == feature, ls_ref[feature], scales)
    own_ref[0:FEAT, :] = pts_ref[...] / scales * SCALE
    own_ref[FEAT:ROWS, :] = prb_ref[...]


def scale(round_index, plan, ls, points, probes):
    vmem, smem = pl.BlockSpec(memory_space=pltpu.VMEM), pl.BlockSpec(memory_space=pltpu.SMEM)
    return pl.pallas_call(
        scale_kernel,
        out_shape=[jax.ShapeDtypeStruct((1,), jnp.int32), jax.ShapeDtypeStruct((ROWS, PTS), F32)],
        in_specs=[smem, smem, smem, vmem, vmem],
        out_specs=[smem, vmem],
        name="scale",
    )(round_index, plan, ls, points, probes)


def swap_kernel(shift, own_ref, far_ref, there_ref, send_sem, recv_sem):
    grp, half, ring, core = coordinates()
    partner = grp
    for bit in range(4):
        if shift >> bit & 1:
            partner = partner + (1 - 2 * ((grp // (1 << bit)) % 2)) * (1 << bit)
    devices = [member(partner, half, ring, core), member(grp, half, ring, 1 - core)]
    barrier = enter(devices)
    pl.semaphore_wait(barrier, len(devices))
    copies = [
        remote(own_ref, far_ref, send_sem.at[0], recv_sem.at[0], devices[0]),
        remote(own_ref.at[0:FEAT], there_ref, send_sem.at[1], recv_sem.at[1], devices[1]),
    ]
    for copy in copies:
        copy.start()
    for copy in copies:
        copy.wait()


def swap(shift, own):
    vmem = pl.BlockSpec(memory_space=pltpu.VMEM)
    return pl.pallas_call(
        functools.partial(swap_kernel, shift),
        out_shape=[jax.ShapeDtypeStruct((ROWS, PTS), F32), jax.ShapeDtypeStruct((FEAT, PTS), F32)],
        in_specs=[vmem],
        out_specs=[vmem] * 2,
        scratch_shapes=[pltpu.SemaphoreType.DMA((2,)), pltpu.SemaphoreType.DMA((2,))],
        compiler_params=pltpu.CompilerParams(collective_id=shift, has_side_effects=True),
        name="swap",
    )(own)


def pieces(x):
    first = x.astype(BF16)
    rest = x - first.astype(F32)
    second = rest.astype(BF16)
    third = (rest - second.astype(F32)).astype(BF16)
    return first, second, third


def lifted(x, left):
    norm = jnp.sum(x * x, axis=0, keepdims=True)
    if left:
        x = x * -2.0
    a, b, c = pieces(x)
    row = lax.broadcasted_iota(jnp.int32, (FEAT, PTS), 0)
    first = 0 if left else 3
    ones = jnp.logical_and(row >= 3 - first, row < 6 - first)
    tail = jnp.where(ones, 1.0, 0.0)
    for index, part in enumerate(pieces(norm)):
        tail = jnp.where(row == first + index, jnp.broadcast_to(part.astype(F32), tail.shape), tail)
    tail = tail.astype(BF16)
    rows = [a, a, b, a, b, c] if left else [a, b, a, c, b, a]
    return jnp.concatenate(rows + [tail, jnp.zeros_like(tail)], 0)


def dot(a, b):
    return lax.dot_general(a, b, (((1,), (0,)), ((), ())), preferred_element_type=F32)


def matern(dist):
    t = jnp.maximum(dist, 1e-30)
    y = t * lax.rsqrt(t) * SLOPE
    return (t - y + SHIFT) * jnp.exp2(y)


OWN, CORE, HALF, BOTH = range(4)
STEPS = (0, 1, -1, 2, -2, 3, -3, 4)
PAIRS = [(OWN, 0), (CORE, 0), (OWN, 1), (CORE, 1), (OWN, 2), (CORE, 2), (CORE, 3)]
PAIRS += [(who, block) for first in (0, 4) for who in (HALF, BOTH) for block in range(first, first + 4)]
PAIRS += [(CORE, block) for block in range(4, RING)]
PAIRS += [(OWN, block) for block in range(3, RING)]
GROUP = 4
GROUPS = len(PAIRS) // GROUP
READY = {1: (3,), 3: (4, 5), 4: (6, 7)}


def block_kernel(
    own_ref, far_ref, there_ref, out_ref,
    land, other, left, right, probes, d0, d1, h0, h1, l0, l1, acc, part, back,
    land_sem, back_sem, ring_sem, part_sem, other_send, other_recv,
):
    grp, half, ring, core = coordinates()

    def place(step):
        return (ring + step + RING) % RING

    around = [member(grp, half, place(step), core) for step in STEPS]
    near = near_devices()
    barrier = enter(around[1:] + near)
    ring_to = [
        remote(far_ref, land.at[ring], ring_sem.at[at - 1], land_sem.at[ring], around[at])
        for at in range(1, RING)
    ]
    half_to = remote(own_ref.at[0:FEAT], other.at[0], other_send.at[0], other_recv.at[0], near[1])
    both_to = remote(other.at[0], other.at[1], other_send.at[1], other_recv.at[1], near[0])
    sums_to = [remote(part.at[at], back.at[at], part_sem.at[at], back_sem.at[at], near[at]) for at in range(3)]

    def block_arrived(at):
        where = place(STEPS[at])
        remote(far_ref, land.at[where], ring_sem.at[0], land_sem.at[where], around[at]).wait_recv()

    D, H, L = (d0, d1), (h0, h1), (l0, l1)

    def lift(at):
        where = place(STEPS[at])
        block = land.at[where] if at else far_ref
        right[where] = lifted(block[0:FEAT, :], False).T
        values = block[FEAT:ROWS, :]
        high = values.astype(BF16)
        probes[where] = jnp.concatenate([high, (values - high.astype(F32)).astype(BF16)], 0)

    def distances(pair, k):
        who, where = pair
        D[k][...] = dot(right[where], left[who])

    def products(pair, k):
        who, where = pair
        acc[who] += dot(probes[where], H[k][...]) + dot(probes[where], L[k][...])

    def step(pair, ahead, behind, k):
        o = 1 - k
        for r in range(0, PTS, 256):
            for c in range(0, PTS, 256):
                rows, cols = slice(r, r + 256), slice(c, c + 256)
                value = matern(D[k][rows, cols])
                high = value.astype(BF16)
                H[k][rows, cols] = high
                L[k][rows, cols] = (value - high.astype(F32)).astype(BF16)
                if ahead is not None:
                    D[o][rows, cols] = dot(right[ahead[1], rows, :], left[ahead[0], :, cols])
                if behind is not None:
                    weights = probes[behind[1], :, rows]
                    acc[behind[0], :, cols] += dot(weights, H[o][rows, cols]) + dot(weights, L[o][rows, cols])

    pairs = [(who, place(STEPS[at])) for who, at in PAIRS]
    left[OWN] = lifted(own_ref[0:FEAT, :], True)
    lift(0)
    distances(pairs[0], 0)
    left[CORE] = lifted(there_ref[...], True)
    acc[...] = jnp.zeros_like(acc)
    step(pairs[0], pairs[1], None, 0)
    step(pairs[1], None, pairs[0], 1)
    pl.semaphore_wait(barrier, RING - 1 + 3)
    ring_to[0].start()
    ring_to[1].start()
    half_to.start()
    for item in ring_to[2:]:
        item.start()
    for at in (1, 2):
        block_arrived(at)
        lift(at)
    distances(pairs[2], 0)
    step(pairs[2], pairs[3], pairs[1], 0)
    step(pairs[3], pairs[4], pairs[2], 1)

    def picked(index, values):
        result = values[0]
        for at in range(1, len(values)):
            result = jnp.where(index == at, values[at], result)
        return result

    whos = [who for who, _ in PAIRS]
    wheres = [where for _, where in pairs]

    def pair_at(n, q):
        at = [min(g * GROUP + q, len(PAIRS) - 1) for g in range(GROUPS)]
        return picked(n, [whos[i] for i in at]), picked(n, [wheres[i] for i in at])

    def send_sum(who):
        part[who - 1] = acc[who, 0:PROBES, :] + acc[who, PROBES : 2 * PROBES, :]
        sums_to[who - 1].start()

    def body(n, carry):
        for m, blocks_ready in READY.items():
            @pl.when(n == m)
            def _():
                for at in blocks_ready:
                    block_arrived(at)
                    lift(at)

        @pl.when(n == 1)
        def _():
            half_to.wait_recv()
            both_to.start()
            left[HALF] = lifted(other[0], True)

        @pl.when(n == 2)
        def _():
            both_to.wait_recv()
            left[BOTH] = lifted(other[1], True)

        @pl.when(n == 6)
        def _():
            send_sum(HALF)
            send_sum(BOTH)

        @pl.when(n == 7)
        def _():
            send_sum(CORE)

        seq = [pair_at(n, q) for q in range(-1, GROUP + 1)]
        for q in range(GROUP):
            step(seq[q + 1], seq[q + 2], seq[q], q % 2)
        return carry

    lax.fori_loop(1, GROUPS, body, 0)
    products(pairs[-1], 1)
    total = acc[OWN, 0:PROBES, :] + acc[OWN, PROBES : 2 * PROBES, :]
    for who in (HALF, BOTH, CORE):
        sums_to[who - 1].wait_recv()
        total += back[who - 1]
    out_ref[...] = total * (1.0 / SHIFT)
    for item in ring_to + [half_to, both_to] + sums_to:
        item.wait_send()


def blocks(own, far, there):
    vmem = pl.BlockSpec(memory_space=pltpu.VMEM)
    dma = pltpu.SemaphoreType.DMA
    return pl.pallas_call(
        block_kernel,
        out_shape=jax.ShapeDtypeStruct((PROBES, PTS), F32),
        in_specs=[vmem] * 3,
        out_specs=vmem,
        scratch_shapes=[
            pltpu.VMEM((RING, ROWS, PTS), F32),
            pltpu.VMEM((2, FEAT, PTS), F32),
            pltpu.VMEM((4, DEPTH, PTS), BF16),
            pltpu.VMEM((RING, PTS, DEPTH), BF16),
            pltpu.VMEM((RING, 2 * PROBES, PTS), BF16),
            pltpu.VMEM((PTS, PTS), F32),
            pltpu.VMEM((PTS, PTS), F32),
            pltpu.VMEM((PTS, PTS), BF16),
            pltpu.VMEM((PTS, PTS), BF16),
            pltpu.VMEM((PTS, PTS), BF16),
            pltpu.VMEM((PTS, PTS), BF16),
            pltpu.VMEM((4, 2 * PROBES, PTS), F32),
            pltpu.VMEM((3, PROBES, PTS), F32),
            pltpu.VMEM((3, PROBES, PTS), F32),
            dma((RING,)), dma((3,)), dma((RING - 1,)), dma((3,)), dma((2,)), dma((2,)),
        ],
        compiler_params=pltpu.CompilerParams(
            collective_id=0, has_side_effects=True, vmem_limit_bytes=32 << 20
        ),
        name="blocks",
    )(own, far, there)


def shards(points, lengthscales, probes, plan, round_index):
    shift, own = scale(round_index, plan, lengthscales, points, probes)
    far, there = lax.switch(shift[0], [functools.partial(swap, which) for which in range(1, 16)], own)
    return blocks(own, far, there)


def solution(mesh):
    in_specs = (P(None, ("grp", "mem")), P(), P(None, ("grp", "mem")), P(), P())
    out_specs = P(None, ("grp", "mem"))
    return jax.shard_map(shards, mesh=mesh, in_specs=in_specs, out_specs=out_specs, check_vma=False)
```

profile of v0, /device:TPU:1, one launch (start us, length us, event | category | flops | bytes accessed | tf_op | source)
XLA Modules:
  0.0 48.5 jit_solution(13690555661762982875)
XLA Ops:
  0.7 1.3 %scale.1 = (s32[1]{0:T(128)}, f32[24,512]{1,0:T(8,128)S(1)}) custom-call(s32[1]{0:T(128)S(6)} %copy.37.round_ref, s32[16,16]{1,0:T(8,128)} %plan_ref.1, f32[16]{0:T(128)} %ls_ref.1, f32[16,512]{1,0:T(8,128)} %pts_ref.1, f32[8,512]{1,0:T(8,128)} %prb_ref.1), custom_call_target="tpu_custom_call" | custom-call | tf_op jit(solution)/shard_map/scale/pallas_call | solution.py:69
  2.6 11.7 %conditional.1 = ((f32[24,512]{1,0:T(8,128)S(1)}, f32[16,512]{1,0:T(8,128)S(1)})) conditional(s32[]{:T(128)} %bitcast, f32[24,512]{1,0:T(8,128)S(1)} %get-tuple-element.24.own_ref, f32[24,512]{1,0:T(8,128)S(1)} %get-tuple-element.24.own_ref, f32[24,512]{1,0:T(8,128)S(1)} %get-tuple-element.24.own_ref, ...), branch_computations={%region_0.0_spmd, %region_1.0_spmd, %region_2.0_spmd, %region_3.0_... | conditional | bytes 8 | solution.py:329
  2.7 11.7 %swap.29 = (f32[24,512]{1,0:T(8,128)S(1)}, f32[16,512]{1,0:T(8,128)S(1)}) custom-call(f32[24,512]{1,0:T(8,128)S(1)} %own_ref.14), custom_call_target="tpu_custom_call" | custom-call | tf_op jit(solution)/shard_map/cond/branch_14_fun/swap/pallas_call | solution.py:99
  14.4 33.5 %blocks.1 = f32[8,512]{1,0:T(8,128)S(1)} custom-call(f32[24,512]{1,0:T(8,128)S(1)} %get-tuple-element.24.own_ref, f32[24,512]{1,0:T(8,128)S(1)} %get-tuple-element.26.far_ref, f32[16,512]{1,0:T(8,128)S(1)} %get-tuple-element.27.there_ref), custom_call_target="tpu_custom_call" | custom-call | tf_op jit(solution)/shard_map/blocks/pallas_call | solution.py:298
  47.9 0.6 %copy.38 = f32[8,512]{1,0:T(8,128)} copy(f32[8,512]{1,0:T(8,128)S(1)} %blocks.1) | data formatting | bytes 32768
where the time goes:
time: 48.8 us; the launch traced here: 48.5 us
  Pallas kernels  46.5 us (95%)
  between operations  1.32 us (3%)
  local copies, waits for them, and re-layouts  0.61 us (1%)
    pallas_call x1, Pallas kernels, blocks(): pl.pallas_call(block_kernel, out_shape=jax.ShapeDtypeStruct((PROBES, PTS)...  33.5 us
    pallas_call x1, Pallas kernels, swap(): pl.pallas_call(functools.partial(swap_kernel, shift), out_shape=[jax.Shap...  11.7 us
    pallas_call x1, Pallas kernels, scale(): pl.pallas_call(scale_kernel, out_shape=[jax.ShapeDtypeStruct((1,), jnp.in...  1.33 us

commit v1 on v0

--- a/solution.py
+++ b/solution.py
@@ -148,6 +148,7 @@
 PAIRS += [(CORE, block) for block in range(4, RING)]
 PAIRS += [(OWN, block) for block in range(3, RING)]
 GROUP = 4
+TILE, CHUNK = 256, 16
 GROUPS = len(PAIRS) // GROUP
 READY = {1: (3,), 3: (4, 5), 4: (6, 7)}
 
@@ -197,18 +198,23 @@
 
     def step(pair, ahead, behind, k):
         o = 1 - k
-        for r in range(0, PTS, 256):
-            for c in range(0, PTS, 256):
-                rows, cols = slice(r, r + 256), slice(c, c + 256)
-                value = matern(D[k][rows, cols])
-                high = value.astype(BF16)
-                H[k][rows, cols] = high
-                L[k][rows, cols] = (value - high.astype(F32)).astype(BF16)
+        for c in range(0, PTS, TILE):
+            for r in range(0, PTS, TILE):
+                rows, cols = slice(r, r + TILE), slice(c, c + TILE)
                 if ahead is not None:
                     D[o][rows, cols] = dot(right[ahead[1], rows, :], left[ahead[0], :, cols])
-                if behind is not None:
-                    weights = probes[behind[1], :, rows]
-                    acc[behind[0], :, cols] += dot(weights, H[o][rows, cols]) + dot(weights, L[o][rows, cols])
+                for at in range(r, r + TILE, CHUNK):
+                    if at == r + TILE // 2 and behind is not None:
+                        weights = probes[behind[1], :, rows]
+                        acc[behind[0], :, cols] += dot(weights, H[o][rows, cols]) + dot(weights, L[o][rows, cols])
+                    chunk = slice(at, at + CHUNK)
+                    value = matern(D[k][chunk, cols])
+                    high = value.astype(BF16)
+                    H[k][chunk, cols] = high
+                    L[k][chunk, cols] = (value - high.astype(F32)).astype(BF16)
+
+    def region(at, work):
+        pl.when(ring < RING + at)(work)
 
     pairs = [(who, place(STEPS[at])) for who, at in PAIRS]
     left[OWN] = lifted(own_ref[0:FEAT, :], True)
@@ -216,20 +222,20 @@
     distances(pairs[0], 0)
     left[CORE] = lifted(there_ref[...], True)
     acc[...] = jnp.zeros_like(acc)
-    step(pairs[0], pairs[1], None, 0)
-    step(pairs[1], None, pairs[0], 1)
     pl.semaphore_wait(barrier, RING - 1 + 3)
     ring_to[0].start()
     ring_to[1].start()
     half_to.start()
     for item in ring_to[2:]:
         item.start()
+    region(0, lambda: step(pairs[0], pairs[1], None, 0))
+    region(1, lambda: step(pairs[1], None, pairs[0], 1))
     for at in (1, 2):
         block_arrived(at)
         lift(at)
     distances(pairs[2], 0)
-    step(pairs[2], pairs[3], pairs[1], 0)
-    step(pairs[3], pairs[4], pairs[2], 1)
+    region(2, lambda: step(pairs[2], pairs[3], pairs[1], 0))
+    region(3, lambda: step(pairs[3], pairs[4], pairs[2], 1))
 
     def picked(index, values):
         result = values[0]
@@ -278,7 +284,7 @@
 
         seq = [pair_at(n, q) for q in range(-1, GROUP + 1)]
         for q in range(GROUP):
-            step(seq[q + 1], seq[q + 2], seq[q], q % 2)
+            region(n + q, functools.partial(step, seq[q + 1], seq[q + 2], seq[q], q % 2))
         return carry
 
     lax.fori_loop(1, GROUPS, body, 0)

time: 48.8 us -> 44.2 us (0.906)
  Pallas kernels: 46.5 us -> 41.6 us
    pallas_call x1, Pallas kernels: 11.7 us -> 9.03 us  [swap(): pl.pallas_call(functools.partial(swap_kernel, shift), out_shape=[jax.Shap...]
    pallas_call x1, Pallas kernels: 33.5 us -> 31.2 us  [blocks(): pl.pallas_call(block_kernel, out_shape=jax.ShapeDtypeStruct((PROBES, PTS)...]
where the time goes in v1:
time: 44.2 us; the launch traced here: 43.6 us
  Pallas kernels  41.6 us (94%)
  between operations  1.32 us (3%)
  local copies, waits for them, and re-layouts  0.61 us (1%)
    pallas_call x1, Pallas kernels, blocks(): pl.pallas_call(block_kernel, out_shape=jax.ShapeDtypeStruct((PROBES, PTS)...  31.2 us
    pallas_call x1, Pallas kernels, swap(): pl.pallas_call(functools.partial(swap_kernel, shift), out_shape=[jax.Shap...  9.03 us
    pallas_call x1, Pallas kernels, scale(): pl.pallas_call(scale_kernel, out_shape=[jax.ShapeDtypeStruct((1,), jnp.in...  1.33 us

profile of v1, /device:TPU:1, one launch (start us, length us, event | category | flops | bytes accessed | tf_op | source)
XLA Modules:
  0.0 43.6 jit_solution(3771943750584182699)
XLA Ops:
  0.7 1.3 %scale.1 = (s32[1]{0:T(128)}, f32[24,512]{1,0:T(8,128)S(1)}) custom-call(s32[1]{0:T(128)S(6)} %copy.37.round_ref, s32[16,16]{1,0:T(8,128)} %plan_ref.1, f32[16]{0:T(128)} %ls_ref.1, f32[16,512]{1,0:T(8,128)} %pts_ref.1, f32[8,512]{1,0:T(8,128)} %prb_ref.1), custom_call_target="tpu_custom_call" | custom-call | tf_op jit(solution)/shard_map/scale/pallas_call | solution.py:69
  2.6 9.1 %conditional.1 = ((f32[24,512]{1,0:T(8,128)S(1)}, f32[16,512]{1,0:T(8,128)S(1)})) conditional(s32[]{:T(128)} %bitcast, f32[24,512]{1,0:T(8,128)S(1)} %get-tuple-element.24.own_ref, f32[24,512]{1,0:T(8,128)S(1)} %get-tuple-element.24.own_ref, f32[24,512]{1,0:T(8,128)S(1)} %get-tuple-element.24.own_ref, ...), branch_computations={%region_0.0_spmd, %region_1.0_spmd, %region_2.0_spmd, %region_3.0_... | conditional | bytes 8 | solution.py:335
  2.7 9.0 %swap.19 = (f32[24,512]{1,0:T(8,128)S(1)}, f32[16,512]{1,0:T(8,128)S(1)}) custom-call(f32[24,512]{1,0:T(8,128)S(1)} %own_ref.4), custom_call_target="tpu_custom_call" | custom-call | tf_op jit(solution)/shard_map/cond/branch_4_fun/swap/pallas_call | solution.py:99
  11.7 31.2 %blocks.1 = f32[8,512]{1,0:T(8,128)S(1)} custom-call(f32[24,512]{1,0:T(8,128)S(1)} %get-tuple-element.24.own_ref, f32[24,512]{1,0:T(8,128)S(1)} %get-tuple-element.26.far_ref, f32[16,512]{1,0:T(8,128)S(1)} %get-tuple-element.27.there_ref), custom_call_target="tpu_custom_call" | custom-call | tf_op jit(solution)/shard_map/blocks/pallas_call | solution.py:304
  43.0 0.6 %copy.38 = f32[8,512]{1,0:T(8,128)} copy(f32[8,512]{1,0:T(8,128)S(1)} %blocks.1) | data formatting | bytes 32768

commit v2 on v1

--- a/solution.py
+++ b/solution.py
@@ -143,14 +143,15 @@
 
 OWN, CORE, HALF, BOTH = range(4)
 STEPS = (0, 1, -1, 2, -2, 3, -3, 4)
-PAIRS = [(OWN, 0), (CORE, 0), (OWN, 1), (CORE, 1), (OWN, 2), (CORE, 2), (CORE, 3)]
-PAIRS += [(who, block) for first in (0, 4) for who in (HALF, BOTH) for block in range(first, first + 4)]
-PAIRS += [(CORE, block) for block in range(4, RING)]
+PAIRS = [(OWN, 0), (CORE, 0), (OWN, 1), (CORE, 1), (OWN, 2), (CORE, 2)]
+PAIRS += [(who, block) for who in (HALF, BOTH) for block in range(4)]
+PAIRS += [(who, block) for first in (4, 6) for who in (HALF, BOTH) for block in range(first, first + 2)]
+PAIRS += [(CORE, block) for block in range(3, RING)]
 PAIRS += [(OWN, block) for block in range(3, RING)]
 GROUP = 4
 TILE, CHUNK = 256, 16
 GROUPS = len(PAIRS) // GROUP
-READY = {1: (3,), 3: (4, 5), 4: (6, 7)}
+READY = {2: (3,), 3: (4, 5), 4: (6, 7)}
 
 
 def block_kernel(

time: 44.2 us -> 43.4 us (0.982); the launches traced: 43.6 us -> 44.1 us
  Pallas kernels: 41.6 us -> 42.2 us
where the time goes in v2:
time: 43.4 us; the launch traced here: 44.1 us
  Pallas kernels  42.2 us (97%)
  between operations  1.32 us (3%)
  local copies, waits for them, and re-layouts  0.61 us (1%)
    pallas_call x1, Pallas kernels, blocks(): pl.pallas_call(block_kernel, out_shape=jax.ShapeDtypeStruct((PROBES, PTS)...  31.4 us
    pallas_call x1, Pallas kernels, swap(): pl.pallas_call(functools.partial(swap_kernel, shift), out_shape=[jax.Shap...  9.46 us
    pallas_call x1, Pallas kernels, scale(): pl.pallas_call(scale_kernel, out_shape=[jax.ShapeDtypeStruct((1,), jnp.in...  1.33 us

profile of v2, /device:TPU:1, one launch (start us, length us, event | category | flops | bytes accessed | tf_op | source)
XLA Modules:
  0.0 44.1 jit_solution(7841827494414967865)
XLA Ops:
  0.7 1.3 %scale.1 = (s32[1]{0:T(128)}, f32[24,512]{1,0:T(8,128)S(1)}) custom-call(s32[1]{0:T(128)S(6)} %copy.37.round_ref, s32[16,16]{1,0:T(8,128)} %plan_ref.1, f32[16]{0:T(128)} %ls_ref.1, f32[16,512]{1,0:T(8,128)} %pts_ref.1, f32[8,512]{1,0:T(8,128)} %prb_ref.1), custom_call_target="tpu_custom_call" | custom-call | tf_op jit(solution)/shard_map/scale/pallas_call | solution.py:69
  2.6 9.5 %conditional.1 = ((f32[24,512]{1,0:T(8,128)S(1)}, f32[16,512]{1,0:T(8,128)S(1)})) conditional(s32[]{:T(128)} %bitcast, f32[24,512]{1,0:T(8,128)S(1)} %get-tuple-element.24.own_ref, f32[24,512]{1,0:T(8,128)S(1)} %get-tuple-element.24.own_ref, f32[24,512]{1,0:T(8,128)S(1)} %get-tuple-element.24.own_ref, ...), branch_computations={%region_0.0_spmd, %region_1.0_spmd, %region_2.0_spmd, %region_3.0_... | conditional | bytes 8 | solution.py:336
  2.7 9.5 %swap.17 = (f32[24,512]{1,0:T(8,128)S(1)}, f32[16,512]{1,0:T(8,128)S(1)}) custom-call(f32[24,512]{1,0:T(8,128)S(1)} %own_ref.2), custom_call_target="tpu_custom_call" | custom-call | tf_op jit(solution)/shard_map/cond/branch_2_fun/swap/pallas_call | solution.py:99
  12.2 31.4 %blocks.1 = f32[8,512]{1,0:T(8,128)S(1)} custom-call(f32[24,512]{1,0:T(8,128)S(1)} %get-tuple-element.24.own_ref, f32[24,512]{1,0:T(8,128)S(1)} %get-tuple-element.26.far_ref, f32[16,512]{1,0:T(8,128)S(1)} %get-tuple-element.27.there_ref), custom_call_target="tpu_custom_call" | custom-call | tf_op jit(solution)/shard_map/blocks/pallas_call | solution.py:305
  43.5 0.6 %copy.38 = f32[8,512]{1,0:T(8,128)} copy(f32[8,512]{1,0:T(8,128)S(1)} %blocks.1) | data formatting | bytes 32768
